TPU v7x, 256 devices: a whole 4x4x8 slice. The times are simulated.
256 devices in a mesh: row: 64 (over y, z, core), col: 4 (over x).
Axes of the slice: x: 4, y: 4, z: 8, core: 2. Of those that a mesh axis runs over, the one named last changes fastest.
Arguments:
- matrix: float32 [262144, 1024], P('row', 'col'), may hold values from -6 to 6
- signs: int32 [262144], P('row'), may hold values from -1 to 1, as said below
- samples: int32 [4096], replicated, may hold values from 0 to 262143, as said below
Outputs:
- sketch: float32 [4096, 1024], P('row', 'col')
- gram: float32 [1024, 1024], P('col')
Inputs may be any that keep to these rules, and one draw needn't show every extreme that they name: `signs`: each entry is +1 or -1. `samples`: for every k, the entries k * 64 to (k + 1) * 64 - 1 are strictly increasing; a row number may appear in several such ranges.
All inputs are finite; a program needn't handle non-finite values.
Results may differ from a plain program's by a relative error of at most 0.00012.
Values sent between devices are 32-bit elements; how exact they have to be, the bound alone decides.
A program may use at most 64 MiB of HBM per device.

v0:
```python
import math

import jax
import jax.numpy as jnp
from jax import lax
from jax.sharding import PartitionSpec as P


def swapped(block, axis, apart):
    count = lax.axis_size(axis)
    route = []
    for low in range(count):
        high = low | 1 << apart
        if high != low and high < count:
            route += [(low, high), (high, low)]
    return lax.ppermute(block, axis, route)


def sign_table(count):
    left = jnp.arange(count, dtype=jnp.int32)[:, None]
    right = jnp.arange(count, dtype=jnp.int32)[None, :]
    parity = jnp.zeros((count, count), jnp.int32)
    for level in range(count.bit_length() - 1):
        parity = parity + left // 2**level % 2 * (right // 2**level % 2)
    return (1 - 2 * (parity % 2)).astype(jnp.float32)


def local_transform(block):
    count, width = block.shape
    levels = count.bit_length() - 1
    first = 1 << levels // 2
    second = count // first
    cube = block.reshape(first, second, width)
    cube = jnp.einsum("ij,jkc->ikc", sign_table(first), cube, precision=lax.Precision.HIGHEST)
    cube = jnp.einsum("kl,ilc->ikc", sign_table(second), cube, precision=lax.Precision.HIGHEST)
    return cube.reshape(count, width)


def scatter_rows(term, share):
    return lax.psum_scatter(
        term(jnp.int32(0), share * lax.axis_size("row")), "row", scatter_dimension=0, tiled=True
    )


def body(matrix, signs, samples):
    rows, width = matrix.shape
    groups = lax.axis_size("row")
    mine = lax.axis_index("row")
    scale = 1.0 / math.sqrt(rows * groups)
    signed = matrix * signs.astype(jnp.float32)[:, None]
    local = local_transform(signed)
    block_of = samples // rows
    inner = samples % rows
    share = samples.shape[0] // groups
    current = local
    for level in range(groups.bit_length() - 1):
        partner = swapped(current, "row", level)
        upper = mine // 2**level % 2
        current = jnp.where(upper == 1, partner - current, current + partner)

    def term(start, count):
        picked = jnp.take(current, inner, axis=0)
        return jnp.where((block_of == mine)[:, None], picked * scale, 0.0)

    sketch = scatter_rows(term, share)
    whole = lax.all_gather(sketch, "col", axis=1, tiled=True)
    partial_gram = (
        jnp.dot(
            sketch.T, whole, precision=lax.Precision.HIGHEST, preferred_element_type=jnp.float32
        )
        / samples.shape[0]
    )
    gram = lax.psum(partial_gram, "row")
    return (sketch, gram)


def solution(mesh):
    return jax.shard_map(
        body,
        mesh=mesh,
        in_specs=(P("row", "col"), P("row"), P()),
        out_specs=(P("row", "col"), P("col", None)),
        check_vma=False,
    )
```

profile of v0, /device:TPU:1, one launch (start us, length us, event | category | flops | bytes accessed | tf_op | source)
XLA Modules:
  0.0 1091.8 jit_solution(14519590833084357724)
XLA Ops:
  7.2 0.0 reduce-scatter.2.cloned.1.call-start
  7.2 0.7 convert_element_type.10
  8.0 2.6 broadcast_multiply_fusion
  10.5 6.2 fusion.2
  16.7 7.1 fusion
  23.8 3.2 collective-permute-start
  27.1 7.1 collective-permute-done
  34.2 6.0 add_select_fusion.5
  40.2 0.0 collective-permute-start.1
  40.2 92.1 %collective-permute-done.1 = f32[4096,256]{1,0:T(8,128)} collective-permute-done((f32[4096,256]{1,0:T(8,128)}, f32[4096,256]{1,0:T(8,128)}, u32[]{:S(2)}, u32[]{:S(2)}) %collective-permute-start.1) | collective-permute-done | bytes 4194336 | tf_op jit(solution)/shard_map/ppermute | solution.py:16
  132.3 6.0 add_select_fusion.4
  138.2 1.6 collective-permute-start.2
  139.8 181.7 %collective-permute-done.2 = f32[4096,256]{1,0:T(8,128)} collective-permute-done((f32[4096,256]{1,0:T(8,128)}, f32[4096,256]{1,0:T(8,128)}, u32[]{:S(2)}, u32[]{:S(2)}) %collective-permute-start.2) | collective-permute-done | bytes 4194336 | tf_op jit(solution)/shard_map/ppermute | solution.py:16
  321.6 6.0 add_select_fusion.3
  327.5 4.9 collective-permute-start.3
  332.4 181.3 %collective-permute-done.3 = f32[4096,256]{1,0:T(8,128)} collective-permute-done((f32[4096,256]{1,0:T(8,128)}, f32[4096,256]{1,0:T(8,128)}, u32[]{:S(2)}, u32[]{:S(2)}) %collective-permute-start.3) | collective-permute-done | bytes 4194336 | tf_op jit(solution)/shard_map/ppermute | solution.py:16
  513.8 6.0 add_select_fusion.2
  519.7 0.9 collective-permute-start.4
  520.6 0.0 copy-start
  520.6 89.8 %collective-permute-done.4 = f32[4096,256]{1,0:T(8,128)} collective-permute-done((f32[4096,256]{1,0:T(8,128)}, f32[4096,256]{1,0:T(8,128)}, u32[]{:S(2)}, u32[]{:S(2)}) %collective-permute-start.4) | collective-permute-done | bytes 4194336 | tf_op jit(solution)/shard_map/ppermute | solution.py:16
  610.4 6.0 add_select_fusion.1
  616.4 2.5 collective-permute-start.5
  618.9 0.0 copy-done
  619.0 88.7 %collective-permute-done.5 = f32[4096,256]{1,0:T(8,128)} collective-permute-done((f32[4096,256]{1,0:T(8,128)}, f32[4096,256]{1,0:T(8,128)}, u32[]{:S(2)}, u32[]{:S(2)}) %collective-permute-start.5) | collective-permute-done | bytes 4194336 | tf_op jit(solution)/shard_map/ppermute | solution.py:16
  707.7 6.0 add_select_fusion
  713.6 18.3 %gather_fusion = f32[4096,256]{1,0:T(8,128)} fusion(f32[4096,256]{1,0:T(8,128)} %add_select_fusion, s32[4096]{0:T(1024)S(1)} %broadcast_clamp_fusion), kind=kCustom, calls=%fused_computation | custom fusion | bytes 8404992 | tf_op jit(solution)/shard_map/jit(_take)/gather | solution.py:62
  731.9 6.8 multiply_select_fusion
  738.7 0.0 reduce-scatter.2.cloned.1.call-update
  738.7 0.0 all-reduce.2.cloned.1.call-start
  738.8 141.7 %reduce-scatter.2.cloned.1.call-done = f32[64,256]{1,0:T(8,128)} async-done(((f32[4096,256]{1,0:T(8,128)}), f32[64,256]{1,0:T(8,128)}) %reduce-scatter.2.cloned.1.call-update) | async-done | bytes 65552 | tf_op jit(solution)/shard_map/reduce_scatter | solution.py:40
  880.5 9.7 all_gather.3
  890.2 2.8 convolution_multiply_fusion
  893.1 0.0 all-reduce.2.cloned.1.call-update
  893.1 189.6 %all-reduce.2.cloned.1.call-done = f32[256,1024]{1,0:T(8,128)} async-done(((f32[256,1024]{1,0:T(8,128)}), f32[256,1024]{1,0:T(8,128)}) %all-reduce.2.cloned.1.call-update) | async-done | bytes 1048592 | tf_op jit(solution)/shard_map/psum | solution.py:73
  1082.7 2.3 copy.12
  (5 shorter events, 0.1 us)
Async XLA Ops:
  7.2 873.4 %reduce-scatter.2.cloned.1.call-start = ((), (), s32[]{:S(2)}) async-start(), calls=%async_computation.1 | async-start | bytes 4259840 | tf_op jit(solution)/shard_map/reduce_scatter | solution.py:40
  23.8 10.4 collective-permute-start
  40.2 92.1 %collective-permute-start.1 = (f32[4096,256]{1,0:T(8,128)}, f32[4096,256]{1,0:T(8,128)}, u32[]{:S(2)}, u32[]{:S(2)}) collective-permute-start(f32[4096,256]{1,0:T(8,128)} %add_select_fusion.5), channel_id=1, source_target_pairs={{0,8},{8,0},{4,12},{12,4},{16,24},{24,16},{20,28},{28,20},{32,40},... | collective-permute-start | bytes 12582920 | tf_op jit(solution)/shard_map/ppermute | solution.py:16
  138.2 183.3 %collective-permute-start.2 = (f32[4096,256]{1,0:T(8,128)}, f32[4096,256]{1,0:T(8,128)}, u32[]{:S(2)}, u32[]{:S(2)}) collective-permute-start(f32[4096,256]{1,0:T(8,128)} %add_select_fusion.4), channel_id=1, source_target_pairs={{0,16},{16,0},{4,20},{20,4},{8,24},{24,8},{12,28},{28,12},{32,48},... | collective-permute-start | bytes 12582920 | tf_op jit(solution)/shard_map/ppermute | solution.py:16
  327.5 186.2 %collective-permute-start.3 = (f32[4096,256]{1,0:T(8,128)}, f32[4096,256]{1,0:T(8,128)}, u32[]{:S(2)}, u32[]{:S(2)}) collective-permute-start(f32[4096,256]{1,0:T(8,128)} %add_select_fusion.3), channel_id=1, source_target_pairs={{0,32},{32,0},{4,36},{36,4},{8,40},{40,8},{12,44},{44,12},{16,48},... | collective-permute-start | bytes 12582920 | tf_op jit(solution)/shard_map/ppermute | solution.py:16
  519.7 90.7 %collective-permute-start.4 = (f32[4096,256]{1,0:T(8,128)}, f32[4096,256]{1,0:T(8,128)}, u32[]{:S(2)}, u32[]{:S(2)}) collective-permute-start(f32[4096,256]{1,0:T(8,128)} %add_select_fusion.2), channel_id=1, source_target_pairs={{0,64},{64,0},{4,68},{68,4},{8,72},{72,8},{12,76},{76,12},{16,80},... | collective-permute-start | bytes 12582920 | tf_op jit(solution)/shard_map/ppermute | solution.py:16
  520.6 98.3 %copy-start = (s32[4096]{0:T(1024)S(1)}, s32[4096]{0:T(1024)}, u32[]{:S(2)}) copy-start(s32[4096]{0:T(1024)} %param.5) | copy-start | bytes 49156
  616.4 91.3 %collective-permute-start.5 = (f32[4096,256]{1,0:T(8,128)}, f32[4096,256]{1,0:T(8,128)}, u32[]{:S(2)}, u32[]{:S(2)}) collective-permute-start(f32[4096,256]{1,0:T(8,128)} %add_select_fusion.1), channel_id=1, source_target_pairs={{0,128},{128,0},{4,132},{132,4},{8,136},{136,8},{12,140},{140,12},... | collective-permute-start | bytes 12582920 | tf_op jit(solution)/shard_map/ppermute | solution.py:16
  738.7 343.9 %all-reduce.2.cloned.1.call-start = ((), (), s32[]{:S(2)}) async-start(), calls=%async_computation.2 | async-start | bytes 2097152 | tf_op jit(solution)/shard_map/psum | solution.py:73
Sparse Core Ops, SparseCore 0:
  738.9 141.6 reduce-scatter.1
  893.2 189.4 all-reduce.1
where the time goes:
time: 1090 us
  waiting for transfers between devices  972 us (89%)
  other arithmetic  45.9 us (4%)
  local copies, waits for them, and re-layouts  20.6 us (2%)
  matrix products  16.1 us (1%)
  between operations  14.1 us (1%)
  starting transfers between devices  13.2 us (1%)
    ppermute x6, waiting for transfers between devices, swapped(): return lax.ppermute(block, axis, route)  641 us
    psum x1, waiting for transfers between devices, body(): gram = lax.psum(partial_gram, 'row')  190 us
    reduce_scatter x1, waiting for transfers between devices, scatter_rows(): lax.psum_scatter(term(jnp.int32(0), share * lax.axis_size('row')), 'row',...  142 us
    select_n x6, other arithmetic, body(): current = jnp.where(upper == 1, partner - current, current + partner)  35.8 us
  transfers between devices with their start and end apart: 8, of which 8 were waited for; matrix products, arithmetic and copies ran while one was open for 0% of the time, Pallas kernels for 0%

commit v1 on v0

v1 whole, which is shorter than its diff:
```python
import jax
import jax.numpy as jnp
from jax import lax
from jax.experimental import pallas as pl
from jax.experimental.pallas import tpu as pltpu
from jax.sharding import PartitionSpec as P

MESH = pl.DeviceIdType.MESH
NX, NY, NZ = 4, 4, 8
CHIPS = NY * NZ
BLOCK = 4096
GROUP = 256
GROUPS = BLOCK // GROUP
SHARE = 128
LANES = 128
CHUNK = 512


def device(x, y, z, c):
    return (y * (NZ * 2) + z * 2 + c, x)


def parity(bits):
    bits = bits ^ (bits >> 4)
    bits = bits ^ (bits >> 2)
    bits = bits ^ (bits >> 1)
    return bits & 1


def stride(p):
    return (NZ - p) // 2 * (2 * (p % 2) - 1)


def split(values):
    high = values.astype(jnp.bfloat16)
    low = (values - high.astype(jnp.float32)).astype(jnp.bfloat16)
    return high, low


def rows(start, count):
    return pl.ds(pl.multiple_of(start, 8), count)


def kernel(
    matrix, signs, samples, sketch, gram,
    xbuf, ybuf, table, picks, places, mine, other, theirs,
    long1, long2, short1, zpart, total, left, right, skin, block, zgram,
    load_sem, place_sem, core_sem, l1_sem, l2_sem, s1_sem, z_sem, sk_sem,
    row_sem, col_sem, fwd_sem, rs_sem, ag_sem, yag_sem, sib_sem, send_sem,
):
    row = lax.axis_index("row")
    x = lax.axis_index("col")
    y, z, c = row // (NZ * 2), row // 2 % NZ, row % 2
    sibling = device(x, y, z, 1 - c)
    ahead = 1 - 2 * c
    diagonal = (x == y).astype(jnp.int32)

    def at_y(step):
        return device(x, (y + step + NY) % NY, z, c)

    def at_z(step):
        return device(x, y, (z + step + NZ) % NZ, c)

    def load(i):
        part = pl.ds(i * CHUNK, CHUNK)
        return pltpu.make_async_copy(matrix.at[part], xbuf.at[part], load_sem.at[i])

    def send(src, dst, sem, where, slot):
        pltpu.make_async_remote_copy(
            src, dst, send_sem.at[slot], sem, device_id=where, device_id_type=MESH
        ).start()

    def landed(ref, sem):
        pltpu.make_async_copy(ref, ref, sem).wait()

    barrier = pltpu.get_barrier_semaphore()

    def greet(where):
        pl.semaphore_signal(barrier, inc=1, device_id=where, device_id_type=MESH)

    for p in range(NZ - 1):
        greet(at_z(stride(p)))
    for k in range(1, NY):
        greet(at_y(k))
    for k in range(NY):
        if_self = jnp.logical_and(diagonal == 1, y == k)

        @pl.when(jnp.logical_not(if_self))
        def _():
            greet(device(y, k, z, c))

    greet(sibling)
    for i in range(BLOCK // CHUNK):
        load(i).start()

    spots = samples[...]
    flips = parity((spots // BLOCK) & row)
    picks[...] = spots % BLOCK + flips * (2 * BLOCK)
    place = pltpu.make_async_copy(picks, places, place_sem)
    place.start()

    line = lax.broadcasted_iota(jnp.int32, (GROUP, GROUP), 0)
    column = lax.broadcasted_iota(jnp.int32, (GROUP, GROUP), 1)
    hadamard = (1 - 2 * parity(line & column)).astype(jnp.float32) * (1.0 / 512.0)

    def mix(i, _):
        load(i).wait()
        for half in range(CHUNK // GROUP):
            g = i * (CHUNK // GROUP) + half
            sign = jnp.concatenate(
                [signs[pl.ds(2 * g, 1), :], signs[pl.ds(2 * g + 1, 1), :]], axis=1
            ).astype(jnp.float32)
            signed = (hadamard * sign).astype(jnp.bfloat16)
            part = rows(g * GROUP, GROUP)
            high, low = split(xbuf[part, :])
            ybuf[part, :] = jnp.dot(
                signed, high, preferred_element_type=jnp.float32
            ) + jnp.dot(signed, low, preferred_element_type=jnp.float32)
        return 0

    lax.fori_loop(0, BLOCK // CHUNK, mix, 0)

    def fold(t, _):
        for half in range(2):
            lanes = slice(half * LANES, (half + 1) * LANES)
            vals = [ybuf[rows(g * GROUP + t * 8, 8), lanes] for g in range(GROUPS)]
            step = 1
            while step < GROUPS:
                for g in range(GROUPS):
                    if g & step == 0:
                        a, b = vals[g], vals[g + step]
                        vals[g], vals[g + step] = a + b, a - b
                step *= 2
            place_of = jnp.where(c == half, 0, BLOCK)
            for g in range(GROUPS):
                spot = place_of + g * GROUP + t * 8
                table[rows(spot, 8), :] = vals[g]
                table[rows(spot + 2 * BLOCK, 8), :] = -vals[g]
        return 0

    lax.fori_loop(0, GROUP // 8, fold, 0)
    place.wait()
    pl.semaphore_wait(barrier, NZ + NY + NY - 1 - diagonal)

    def chunk(yy, zz):
        return yy * NZ + zz

    def part_of(spot):
        return rows(spot * SHARE, SHARE)

    def gather(spot):
        for base in range(0, SHARE, 16):
            at = [places[spot, base + u] for u in range(16)]
            kept = [table[pl.ds(at[u], 1), :] for u in range(16)]
            given = [table[pl.ds(at[u] + BLOCK, 1), :] for u in range(16)]
            for u in range(16):
                mine[pl.ds(spot * SHARE + base + u, 1), :] = kept[u]
            for u in range(16):
                other[pl.ds(spot * SHARE + base + u, 1), :] = given[u]

    def y_of(q):
        step = jnp.where(q == 0, 2, jnp.where(q == 1, ahead, jnp.where(q == 2, -ahead, 0)))
        return (y + step + NY) % NY

    def z_of(p):
        return (z + stride(p) + NZ) % NZ

    def pick(p):
        def each(q, _):
            spot = chunk(y_of(q), z_of(p))
            gather(spot)
            send(other.at[part_of(spot)], theirs.at[part_of(spot)], core_sem.at[spot], sibling, 0)
            return 0

        lax.fori_loop(0, 4, each, 0)

    def merge(p):
        def each(q, _):
            spot = chunk(y_of(q), z_of(p))
            landed(theirs.at[part_of(spot)], core_sem.at[spot])
            mine[part_of(spot), :] += theirs[part_of(spot), :]
            return 0

        lax.fori_loop(0, 4, each, 0)
        slot = part_of(p)
        far = part_of(chunk(y_of(0), z_of(p)))
        send(mine.at[far], long1.at[slot], l1_sem.at[p], at_y(ahead), 1)
        near = part_of(chunk(y_of(2), z_of(p)))
        send(mine.at[near], short1.at[slot], s1_sem.at[p], at_y(-ahead), 1)

    def second(p):
        slot = part_of(p)
        near = part_of(chunk(y_of(1), z_of(p)))
        landed(long1.at[slot], l1_sem.at[p])
        mine[near, :] += long1[slot, :]
        send(mine.at[near], long2.at[slot], l2_sem.at[p], at_y(ahead), 1)

    def third(p):
        slot = part_of(p)
        own = part_of(chunk(y, z_of(p)))
        landed(short1.at[slot], s1_sem.at[p])
        landed(long2.at[slot], l2_sem.at[p])
        mine[own, :] += short1[slot, :] + long2[slot, :]

        @pl.when(p < NZ - 1)
        def _():
            send(mine.at[own], zpart.at[slot], z_sem.at[p], at_z(stride(p)), 2)

    def turn(t, _):
        @pl.when(t < NZ)
        def _():
            pick(t)
            merge(t)

        @pl.when(jnp.logical_and(t >= 2, t < NZ + 2))
        def _():
            second(t - 2)

        @pl.when(t >= 4)
        def _():
            third(t - 4)

        return 0

    lax.fori_loop(0, NZ + 4, turn, 0)

    home = part_of(chunk(y, z))
    for p in range(NZ - 1):
        landed(zpart.at[part_of(p)], z_sem.at[p])
    total[...] = mine[home, :] + sum(zpart[part_of(p), :] for p in range(NZ - 1))

    slot_y = part_of(y)
    slot_cy = part_of(c * NY + y)
    for j in range(NY - 1, -1, -1):
        xx = (x + j) % NX
        if j == 0:
            @pl.when(diagonal == 1)
            def _():
                right[slot_cy, :] = total[...]

            @pl.when(diagonal == 0)
            def _():
                send(total, right.at[slot_cy], col_sem.at[y], device(xx, x, z, c), 3)
        else:
            send(total, right.at[slot_cy], col_sem.at[y], device(xx, x, z, c), 3)
    for k in (2, 1, 3):
        send(total, left.at[slot_y], row_sem.at[y], at_y(k), 4)
    send(total.at[rows((1 - c) * 64, 64)], skin, sk_sem, sibling, 5)
    left[slot_y, :] = total[...]
    sketch[:, pl.ds(pl.multiple_of(c * LANES, LANES), LANES)] = total[rows(c * 64, 64), :]

    for k in range(NY):
        ys = (y + k) % NY
        spot = part_of(c * NY + ys)
        if k == 0:
            @pl.when(diagonal == 0)
            def _():
                landed(right.at[spot], col_sem.at[ys])
        else:
            landed(right.at[spot], col_sem.at[ys])
        send(right.at[spot], right.at[spot], fwd_sem.at[ys], sibling, 6)
    for k in range(1, NY):
        ys = (y + k) % NY
        landed(left.at[part_of(ys)], row_sem.at[ys])

    lhigh, llow = split(left[...])

    def product(h):
        rhigh, rlow = split(right[rows(h * (NY * SHARE), NY * SHARE), :])
        dims = (((0,), (0,)), ((), ()))
        out = lax.dot_general(lhigh, rhigh, dims, preferred_element_type=jnp.float32)
        out += lax.dot_general(lhigh, rlow, dims, preferred_element_type=jnp.float32)
        out += lax.dot_general(llow, rhigh, dims, preferred_element_type=jnp.float32)
        block[:, pl.ds(pl.multiple_of(h * LANES, LANES), LANES)] = out * (1.0 / 4096.0)

    product(c)
    landed(skin, sk_sem)
    sketch[:, pl.ds(pl.multiple_of((1 - c) * LANES, LANES), LANES)] = skin[...]
    for k in range(NY):
        landed(right.at[part_of((1 - c) * NY + k)], fwd_sem.at[k])
    product(1 - c)

    def strip(zz):
        return rows(zz * 16, 16)

    for p in range(NZ - 1):
        send(block.at[strip(z_of(p))], zgram.at[strip(p)], rs_sem.at[p], at_z(stride(p)), 7)
    acc = block[strip(z), :]
    for p in range(NZ - 2, -1, -1):
        landed(zgram.at[strip(p)], rs_sem.at[p])
        acc = acc + zgram[strip(p), :]

    def tile(cc, zz, yy, count):
        return gram.at[rows(cc * 128 + zz * 16, count), pl.ds(pl.multiple_of(yy * 256, 256), 256)]

    tile_mine = tile(c, z, y, 16)
    tile_mine[...] = acc
    for p in range(NZ - 1):
        send(tile_mine, tile_mine, ag_sem.at[p], at_z(stride(p)), 8)

    def spread(zz):
        piece = tile(c, zz, y, 16)
        for k in (2, 1, 3):
            send(piece, piece, yag_sem.at[k, zz], at_y(k), 9)

    spread(z)
    for p in range(NZ - 2, -1, -1):
        zz = (z - stride(p) + NZ) % NZ
        landed(tile(c, zz, y, 16), ag_sem.at[p])
        spread(zz)
    whole = tile(c, 0, y, 128)
    send(whole, whole, sib_sem.at[y], sibling, 10)
    for k in (1, 3, 2):
        ys = (y - k + NY) % NY
        for zz in range(NZ):
            landed(tile(c, zz, ys, 16), yag_sem.at[k, zz])
        whole = tile(c, 0, ys, 128)
        send(whole, whole, sib_sem.at[ys], sibling, 10)

    def left_here(ref, slot):
        pltpu.make_async_copy(ref, ref, send_sem.at[slot]).wait()

    left_here(other, 0)
    left_here(mine.at[pl.ds(0, 3 * NZ * SHARE)], 1)
    left_here(mine.at[pl.ds(0, (NZ - 1) * SHARE)], 2)

    @pl.when(diagonal == 1)
    def _():
        left_here(mine.at[pl.ds(0, 3 * SHARE)], 3)

    @pl.when(diagonal == 0)
    def _():
        left_here(mine.at[pl.ds(0, 4 * SHARE)], 3)

    left_here(mine.at[pl.ds(0, 3 * SHARE)], 4)
    left_here(mine.at[pl.ds(0, 64)], 5)
    left_here(mine.at[pl.ds(0, 4 * SHARE)], 6)
    left_here(gram.at[pl.ds(0, 16 * (NZ - 1)), pl.ds(0, 256)], 7)
    left_here(gram.at[pl.ds(0, 16 * (NZ - 1)), pl.ds(0, 256)], 8)
    left_here(gram.at[pl.ds(0, 128), pl.ds(0, 768)], 9)
    left_here(gram.at[pl.ds(0, 128), :], 10)
    for k in range(NY):
        landed(tile(1 - c, 0, k, 128), sib_sem.at[k])


def body(matrix, signs, samples):
    vmem = pltpu.VMEM
    f32 = jnp.float32
    dma = pltpu.SemaphoreType.DMA
    spec = pl.BlockSpec(memory_space=pltpu.VMEM)
    return pl.pallas_call(
        kernel,
        out_shape=(
            jax.ShapeDtypeStruct((64, 256), f32),
            jax.ShapeDtypeStruct((256, 1024), f32),
        ),
        in_specs=[pl.BlockSpec(memory_space=pl.ANY), spec, spec],
        out_specs=(spec, spec),
        scratch_shapes=[
            vmem((BLOCK, 256), f32),
            vmem((BLOCK, 256), f32),
            vmem((4 * BLOCK, LANES), f32),
            vmem((CHIPS, SHARE), jnp.int32),
            pltpu.SMEM((CHIPS, SHARE), jnp.int32),
            vmem((CHIPS * SHARE, LANES), f32),
            vmem((CHIPS * SHARE, LANES), f32),
            vmem((CHIPS * SHARE, LANES), f32),
            vmem((NZ * SHARE, LANES), f32),
            vmem((NZ * SHARE, LANES), f32),
            vmem((NZ * SHARE, LANES), f32),
            vmem((NZ * SHARE, LANES), f32),
            vmem((SHARE, LANES), f32),
            vmem((NY * SHARE, LANES), f32),
            vmem((2 * NY * SHARE, LANES), f32),
            vmem((64, LANES), f32),
            vmem((SHARE, 256), f32),
            vmem((SHARE, 256), f32),
            dma((BLOCK // CHUNK,)),
            dma,
            dma((CHIPS,)),
            dma((NZ,)),
            dma((NZ,)),
            dma((NZ,)),
            dma((NZ,)),
            dma,
            dma((NY,)),
            dma((NY,)),
            dma((NY,)),
            dma((NZ,)),
            dma((NZ,)),
            dma((NY, NZ)),
            dma((NY,)),
            dma((11,)),
        ],
        compiler_params=pltpu.CompilerParams(
            collective_id=0, has_side_effects=True, vmem_limit_bytes=44 * 2**20
        ),
    )(matrix, signs.reshape(CHIPS, SHARE), samples.reshape(CHIPS, SHARE))


def solution(mesh):
    return jax.shard_map(
        body,
        mesh=mesh,
        in_specs=(P("row", "col"), P("row"), P()),
        out_specs=(P("row", "col"), P("col", None)),
        check_vma=False,
    )
```

time: 1090 us -> 70.8 us (0.06)
  waiting for transfers between devices: 972 us -> 0 us
  Pallas kernels: 0 us -> 64.7 us
  other arithmetic: 45.9 us -> 0 us
  matrix products: 16.1 us -> 0 us
  local copies, waits for them, and re-layouts: 20.6 us -> 5.22 us
  between operations: 14.1 us -> 0.65 us
  starting transfers between devices: 13.2 us -> 0 us
    ppermute x6 -> x0, waiting for transfers between devices: 641 us -> none  [swapped(): return lax.ppermute(block, axis, route)]
    psum x1 -> x0, waiting for transfers between devices: 190 us -> none  [body(): gram = lax.psum(partial_gram, 'row')]
    reduce_scatter x1 -> x0, waiting for transfers between devices: 142 us -> none  [scatter_rows(): lax.psum_scatter(term(jnp.int32(0), share * lax.axis_size('row')), 'row',...]
    pallas_call x0 -> x1, Pallas kernels: none -> 64.7 us  [body(): pl.pallas_call(kernel, out_shape=(jax.ShapeDtypeStruct((64, 256), f32), j...]
    select_n x10 -> x0, other arithmetic: 42.6 us -> none  [the longest x6 35.8 us: body(): current = jnp.where(upper == 1, partner - current, current + partner)]
    gather x1 -> x0, local copies, waits for them, and re-layouts: 18.3 us -> none  [term(): picked = jnp.take(current, inner, axis=0)]
    dot_general x3 -> x0, matrix products: 16.1 us -> none  [the longest x1 7.11 us: local_transform(): jnp.einsum('kl,ilc->ikc', sign_table(second), cube, precision=lax.Precisi...]
    ppermute x6 -> x0, starting transfers between devices: 13.2 us -> none  [swapped(): return lax.ppermute(block, axis, route)]
  transfers between devices with their start and end apart: 8 -> 0, of which waited for: 8 -> 0; matrix products, arithmetic and copies ran while one was open for 0% -> 0% of each run, Pallas kernels for 0% -> 0%
where the time goes in v1:
time: 70.8 us; the launch traced here: 70.5 us
  Pallas kernels  64.7 us (91%)
  local copies, waits for them, and re-layouts  5.22 us (7%)
    pallas_call x1, Pallas kernels, body(): pl.pallas_call(kernel, out_shape=(jax.ShapeDtypeStruct((64, 256), f32), j...  64.7 us
    unnamed x8, local copies, waits for them, and re-layouts  5.22 us

profile of v1, /device:TPU:1, one launch (start us, length us, event | category | flops | bytes accessed | tf_op | source)
XLA Modules:
  0.0 70.5 jit_solution(8401710498315051260)
XLA Ops:
  0.6 0.0 copy-start
  0.6 2.2 %copy-done = f32[4096,256]{1,0:T(8,128)S(1)} copy-done((f32[4096,256]{1,0:T(8,128)S(1)}, f32[4096,256]{1,0:T(8,128)}, u32[]{:S(2)}) %copy-start) | copy-done | bytes 4194328
  2.8 0.0 copy-start.1
  2.8 0.7 %copy-done.1 = s32[4096]{0:T(1024)S(1)} copy-done((s32[4096]{0:T(1024)S(1)}, s32[4096]{0:T(1024)}, u32[]{:S(2)}) %copy-start.1) | copy-done | bytes 16408
  3.5 0.0 copy-start.2
  3.5 0.7 %copy-done.2 = s32[4096]{0:T(1024)S(1)} copy-done((s32[4096]{0:T(1024)S(1)}, s32[4096]{0:T(1024)}, u32[]{:S(2)}) %copy-start.2) | copy-done | bytes 16408
  4.3 64.7 %shard_map.50 = (f32[64,256]{1,0:T(8,128)S(1)}, f32[256,1024]{1,0:T(8,128)S(1)}) custom-call(f32[4096,256]{1,0:T(8,128)S(1)} %copy-done, s32[32,128]{1,0:T(8,128)S(1)} %bitcast.2, s32[32,128]{1,0:T(8,128)S(1)} %bitcast.3), custom_call_target="tpu_custom_call" | custom-call | tf_op jit(solution)/shard_map/pallas_call | solution.py:351
  68.9 0.6 copy.7
  69.6 1.0 %copy.8 = f32[256,1024]{1,0:T(8,128)} copy(f32[256,1024]{1,0:T(8,128)S(1)} %get-tuple-element.5) | data formatting | bytes 2097152
Async XLA Ops:
  0.6 2.2 %copy-start = (f32[4096,256]{1,0:T(8,128)S(1)}, f32[4096,256]{1,0:T(8,128)}, u32[]{:S(2)}) copy-start(f32[4096,256]{1,0:T(8,128)} %matrix.1) | copy-start | bytes 12582916
  2.8 0.7 %copy-start.1 = (s32[4096]{0:T(1024)S(1)}, s32[4096]{0:T(1024)}, u32[]{:S(2)}) copy-start(s32[4096]{0:T(1024)} %param.4) | copy-start | bytes 49156
  3.5 0.7 %copy-start.2 = (s32[4096]{0:T(1024)S(1)}, s32[4096]{0:T(1024)}, u32[]{:S(2)}) copy-start(s32[4096]{0:T(1024)} %param.5) | copy-start | bytes 49156

commit v2 on v1

v2 whole, which is shorter than its diff:
```python
import jax
import jax.numpy as jnp
from jax import lax
from jax.experimental import pallas as pl
from jax.experimental.pallas import tpu as pltpu
from jax.sharding import PartitionSpec as P

MESH = pl.DeviceIdType.MESH
NX, NY, NZ = 4, 4, 8
CHIPS = NY * NZ
BLOCK = 4096
GROUP = 256
GROUPS = BLOCK // GROUP
SHARE = 128
LANES = 128
CHUNK = 512
YROWS = 104
ZROWS = SHARE - YROWS
FINISH = 4
PICK_Z, MERGE_Z, SECOND_Z, THIRD_Z = 1, 2, 5, 8


def device(x, y, z, c):
    return (y * (NZ * 2) + z * 2 + c, x)


def parity(bits):
    bits = bits ^ (bits >> 4)
    bits = bits ^ (bits >> 2)
    bits = bits ^ (bits >> 1)
    return bits & 1


def stride(p):
    return (NZ - p) // 2 * (2 * (p % 2) - 1)


def split(values):
    high = values.astype(jnp.bfloat16)
    low = (values - high.astype(jnp.float32)).astype(jnp.bfloat16)
    return high, low


def rows(start, count):
    return pl.ds(pl.multiple_of(start, 8), count)


def kernel(
    matrix, signs_in, samples_in, sketch, gram,
    xbuf, ybuf, table, signs, samples, picks, places,
    mine, other, theirs, minez, otherz, theirsz,
    ypart, zpart, zin, yin, total, left, right, skin, block, zgram,
    load_sem, place_sem, core_sem, corez_sem, ypart_sem, z_sem, zin_sem, yin_sem,
    sk_sem, row_sem, col_sem, fwd_sem, rs_sem, ag_sem, far_sem, yag_sem, sib_sem, send_sem,
):
    row = lax.axis_index("row")
    x = lax.axis_index("col")
    y, z, c = row // (NZ * 2), row // 2 % NZ, row % 2
    sibling = device(x, y, z, 1 - c)
    ahead = 1 - 2 * c

    def at_y(step):
        return device(x, (y + step + NY) % NY, z, c)

    def at_z(step):
        return device(x, y, (z + step + NZ) % NZ, c)

    def load(i):
        part = pl.ds(i * CHUNK, CHUNK)
        return pltpu.make_async_copy(matrix.at[part], xbuf.at[part], load_sem.at[i])

    def send(src, dst, sem, where, slot):
        pltpu.make_async_remote_copy(
            src, dst, send_sem.at[slot], sem, device_id=where, device_id_type=MESH
        ).start()

    def landed(ref, sem):
        pltpu.make_async_copy(ref, ref, sem).wait()

    barrier = pltpu.get_barrier_semaphore()

    def greet(where):
        pl.semaphore_signal(barrier, inc=1, device_id=where, device_id_type=MESH)

    get_signs = pltpu.make_async_copy(signs_in, signs, place_sem.at[0])
    get_samples = pltpu.make_async_copy(samples_in, samples, place_sem.at[1])
    get_samples.start()
    get_signs.start()
    for i in range(BLOCK // CHUNK):
        load(i).start()

    for p in range(NZ - 1):
        greet(at_z(stride(p)))
    for k in range(1, NY):
        greet(at_y(k))

    @pl.when(x != y)
    def _():
        for k in range(NY):
            greet(device(y, k, z, c))

    greet(sibling)

    get_samples.wait()
    spots = samples[...]
    flips = parity((spots // BLOCK) & row)
    picks[...] = spots % BLOCK + flips * (2 * BLOCK)
    place = pltpu.make_async_copy(picks, places, place_sem.at[2])
    place.start()

    line = lax.broadcasted_iota(jnp.int32, (GROUP, GROUP), 0)
    column = lax.broadcasted_iota(jnp.int32, (GROUP, GROUP), 1)
    hadamard = (1 - 2 * parity(line & column)).astype(jnp.float32) * (1.0 / 512.0)
    get_signs.wait()

    def mix(i, _):
        load(i).wait()
        for half in range(CHUNK // GROUP):
            g = i * (CHUNK // GROUP) + half
            sign = jnp.concatenate(
                [signs[pl.ds(2 * g, 1), :], signs[pl.ds(2 * g + 1, 1), :]], axis=1
            ).astype(jnp.float32)
            signed = (hadamard * sign).astype(jnp.bfloat16)
            part = rows(g * GROUP, GROUP)
            high, low = split(xbuf[part, :])
            ybuf[part, :] = jnp.dot(
                signed, high, preferred_element_type=jnp.float32
            ) + jnp.dot(signed, low, preferred_element_type=jnp.float32)
        return 0

    lax.fori_loop(0, BLOCK // CHUNK, mix, 0)

    def fold(t, _):
        for half in range(2):
            lanes = slice(half * LANES, (half + 1) * LANES)
            vals = [ybuf[rows(g * GROUP + t * 8, 8), lanes] for g in range(GROUPS)]
            step = 1
            while step < GROUPS:
                for g in range(GROUPS):
                    if g & step == 0:
                        a, b = vals[g], vals[g + step]
                        vals[g], vals[g + step] = a + b, a - b
                step *= 2
            place_of = jnp.where(c == half, 0, BLOCK)
            for g in range(GROUPS):
                spot = place_of + g * GROUP + t * 8
                table[rows(spot, 8), :] = vals[g]
                table[rows(spot + 2 * BLOCK, 8), :] = -vals[g]
        return 0

    lax.fori_loop(0, GROUP // 8, fold, 0)
    place.wait()

    def chunk(yy, zz):
        return yy * NZ + zz

    def gather(spot, first, count, kept_to, given_to, base):
        for start in range(0, count, 8):
            at = [places[spot, first + start + u] for u in range(8)]
            kept = [table[pl.ds(at[u], 1), :] for u in range(8)]
            given = [table[pl.ds(at[u] + BLOCK, 1), :] for u in range(8)]
            for u in range(8):
                kept_to[pl.ds(base + start + u, 1), :] = kept[u]
            for u in range(8):
                given_to[pl.ds(base + start + u, 1), :] = given[u]

    def part_y(spot):
        return rows(spot * YROWS, YROWS)

    def part_z(spot):
        return rows(spot * (NY * ZROWS), NY * ZROWS)

    def part_of(spot):
        return rows(spot * SHARE, SHARE)

    def y_of(q):
        return (y + 2 + q) % NY

    def z_of(p):
        return (z + stride(p) + NZ) % NZ

    def turn_z(step):
        return (z + step + NZ) % NZ

    def pick(p):
        def each(q, _):
            spot = chunk(y_of(q), z_of(p))
            gather(spot, 0, YROWS, mine, other, spot * YROWS)
            return 0

        lax.fori_loop(0, 4, each, 0)

    def give(p):
        def each(q, _):
            spot = chunk(y_of(q), z_of(p))
            send(other.at[part_y(spot)], theirs.at[part_y(spot)], core_sem.at[spot], sibling, 0)
            return 0

        lax.fori_loop(0, 4, each, 0)

    def merge(p):
        def each(q, _):
            spot = chunk(y_of(q), z_of(p))
            landed(theirs.at[part_y(spot)], core_sem.at[spot])
            mine[part_y(spot), :] += theirs[part_y(spot), :]
            return 0

        lax.fori_loop(0, 4, each, 0)
        for k in (2, 1, 3):
            spot = chunk((y + k) % NY, z_of(p))
            send(mine.at[part_y(spot)], ypart.at[part_y(k * NZ + p)], ypart_sem.at[k, p], at_y(k), 1)

    def finish(p):
        own = part_y(chunk(y, z_of(p)))
        for k in (1, 3, 2):
            landed(ypart.at[part_y(k * NZ + p)], ypart_sem.at[k, p])
        mine[own, :] += sum(ypart[part_y(k * NZ + p), :] for k in range(1, NY))

        @pl.when(p < NZ - 1)
        def _():
            send(mine.at[own], zpart.at[part_y(p)], z_sem.at[p], at_z(stride(p)), 2)

    def pick_z():
        def each(p, _):
            zz = z_of(p)
            for yy in range(NY):
                gather(chunk(yy, zz), YROWS, ZROWS, minez, otherz, (zz * NY + yy) * ZROWS)
            send(otherz.at[part_z(zz)], theirsz.at[part_z(zz)], corez_sem.at[zz], sibling, 0)
            return 0

        lax.fori_loop(0, NZ, each, 0)

    def send_z(step, slot, hop):
        send(minez.at[part_z(turn_z(step))], zin.at[part_z(slot)], zin_sem.at[slot], at_z(hop), 11)

    def merge_z():
        def each(p, _):
            zz = z_of(p)
            landed(theirsz.at[part_z(zz)], corez_sem.at[zz])
            minez[part_z(zz), :] += theirsz[part_z(zz), :]
            return 0

        lax.fori_loop(0, NZ, each, 0)
        send_z(4, 0, 2 * ahead)
        send_z(3 * ahead, 1, ahead)
        send_z(-3 * ahead, 2, -ahead)
        send_z(ahead, 3, ahead)
        send_z(-ahead, 4, -ahead)

    def take_z(step, slots):
        zz = turn_z(step)
        for slot in slots:
            landed(zin.at[part_z(slot)], zin_sem.at[slot])
        minez[part_z(zz), :] += sum(zin[part_z(slot), :] for slot in slots)

    def second_z():
        take_z(2 * ahead, (0, 1))
        send_z(2 * ahead, 5, 2 * ahead)
        take_z(-2 * ahead, (2,))
        send_z(-2 * ahead, 6, -2 * ahead)

    def third_z():
        take_z(0, (3, 4, 5, 6))
        for k in range(1, NY):
            part = rows((z * NY + (y + k) % NY) * ZROWS, ZROWS)
            slot = rows(k * ZROWS, ZROWS)
            send(minez.at[part], yin.at[slot], yin_sem.at[k], at_y(k), 12)

    pick(0)
    pl.semaphore_wait(barrier, NZ + NY + NX - 2)
    give(0)
    pick(1)
    give(1)

    def turn(t, _):
        @pl.when(t < NZ)
        def _():
            merge(t)

        @pl.when(t < NZ - 2)
        def _():
            pick(t + 2)
            give(t + 2)

        @pl.when(t == PICK_Z)
        def _():
            pick_z()

        @pl.when(t == MERGE_Z)
        def _():
            merge_z()

        @pl.when(t == SECOND_Z)
        def _():
            second_z()

        @pl.when(t == THIRD_Z)
        def _():
            third_z()

        @pl.when(t >= FINISH)
        def _():
            finish(t - FINISH)

        return 0

    lax.fori_loop(0, NZ + FINISH, turn, 0)

    home = part_y(chunk(y, z))
    for k in range(1, NY):
        landed(yin.at[rows(k * ZROWS, ZROWS)], yin_sem.at[k])
    total[pl.ds(YROWS, ZROWS), :] = minez[rows((z * NY + y) * ZROWS, ZROWS), :] + sum(
        yin[rows(k * ZROWS, ZROWS), :] for k in range(1, NY)
    )
    for p in range(NZ - 1):
        landed(zpart.at[part_y(p)], z_sem.at[p])
    total[pl.ds(0, YROWS), :] = mine[home, :] + sum(zpart[part_y(p), :] for p in range(NZ - 1))

    slot_y = part_of(y)
    slot_cy = part_of(c * NY + y)
    for j in (2, 1, 3):
        send(total, right.at[slot_cy], col_sem.at[y], device((x + j) % NX, x, z, c), 3)
    for k in (2, 1, 3):
        send(total, left.at[slot_y], row_sem.at[y], at_y(k), 4)
    send(total.at[rows((1 - c) * 64, 64)], skin, sk_sem, sibling, 5)
    left[slot_y, :] = total[...]
    sketch[:, pl.ds(pl.multiple_of(c * LANES, LANES), LANES)] = total[rows(c * 64, 64), :]

    for k in range(NY):
        ys = (y + k) % NY
        spot = part_of(c * NY + ys)
        if k > 0:
            landed(left.at[part_of(ys)], row_sem.at[ys])

        @pl.when(x == y)
        def _():
            right[spot, :] = left[part_of(ys), :]

        @pl.when(x != y)
        def _():
            landed(right.at[spot], col_sem.at[ys])

        send(right.at[spot], right.at[spot], fwd_sem.at[ys], sibling, 6)

    lhigh, llow = split(left[...])

    def product(h):
        rhigh, rlow = split(right[rows(h * (NY * SHARE), NY * SHARE), :])
        dims = (((0,), (0,)), ((), ()))
        out = lax.dot_general(lhigh, rhigh, dims, preferred_element_type=jnp.float32)
        out += lax.dot_general(lhigh, rlow, dims, preferred_element_type=jnp.float32)
        out += lax.dot_general(llow, rhigh, dims, preferred_element_type=jnp.float32)
        block[:, pl.ds(pl.multiple_of(h * LANES, LANES), LANES)] = out * (1.0 / 4096.0)

    product(c)
    landed(skin, sk_sem)
    sketch[:, pl.ds(pl.multiple_of((1 - c) * LANES, LANES), LANES)] = skin[...]
    for k in range(NY):
        landed(right.at[part_of((1 - c) * NY + k)], fwd_sem.at[k])
    product(1 - c)

    def strip(zz):
        return rows(zz * 16, 16)

    for p in range(NZ - 1):
        send(block.at[strip(z_of(p))], zgram.at[strip(p)], rs_sem.at[p], at_z(stride(p)), 7)
    acc = block[strip(z), :]
    for p in range(NZ - 2, -1, -1):
        landed(zgram.at[strip(p)], rs_sem.at[p])
        acc = acc + zgram[strip(p), :]

    def tile(cc, zz, yy, count):
        return gram.at[rows(cc * 128 + zz * 16, count), pl.ds(pl.multiple_of(yy * 256, 256), 256)]

    tile_mine = tile(c, z, y, 16)
    tile_mine[...] = acc
    send(tile_mine, tile_mine, yag_sem.at[2, z], at_y(2), 9)
    for p in range(NZ - 1):
        send(tile_mine, tile_mine, ag_sem.at[p], at_z(stride(p)), 8)

    def spread(zz):
        piece = tile(c, zz, y, 16)
        for k in (1, 3):
            send(piece, piece, yag_sem.at[k, zz], at_y(k), 9)

    def across(p):
        zz = (z - stride(p) + NZ) % NZ
        landed(tile(c, zz, y, 16), ag_sem.at[p])
        spread(zz)

    spread(z)
    across(6)
    across(5)
    opposite = (y + 2) % NY
    far = tile(c, z, opposite, 16)
    landed(far, yag_sem.at[2, z])
    for p in range(NZ - 1):
        send(far, far, far_sem.at[p], at_z(stride(p)), 13)
    for p in range(NZ - 4, -1, -1):
        across(p)

    def share(yy):
        whole = tile(c, 0, yy, 128)
        send(whole, whole, sib_sem.at[yy], sibling, 10)

    share(y)
    for k in (1, 3):
        ys = (y - k + NY) % NY
        for zz in range(NZ):
            landed(tile(c, zz, ys, 16), yag_sem.at[k, zz])
        share(ys)
    for p in range(NZ - 1):
        landed(tile(c, (z - stride(p) + NZ) % NZ, opposite, 16), far_sem.at[p])
    share(opposite)

    def left_here(ref, slot):
        pltpu.make_async_copy(ref, ref, send_sem.at[slot]).wait()

    left_here(table.at[pl.ds(0, CHIPS * SHARE)], 0)
    left_here(table.at[pl.ds(0, 3 * NZ * YROWS)], 1)
    left_here(table.at[pl.ds(0, (NZ - 1) * YROWS)], 2)
    left_here(table.at[pl.ds(0, 7 * NY * ZROWS)], 11)
    left_here(table.at[pl.ds(0, (NY - 1) * ZROWS)], 12)

    left_here(table.at[pl.ds(0, 3 * SHARE)], 3)
    left_here(table.at[pl.ds(0, 3 * SHARE)], 4)
    left_here(table.at[pl.ds(0, 64)], 5)
    left_here(table.at[pl.ds(0, 4 * SHARE)], 6)
    left_here(xbuf.at[pl.ds(0, 16 * (NZ - 1))], 7)
    left_here(xbuf.at[pl.ds(0, 16 * (NZ - 1))], 8)
    left_here(xbuf.at[pl.ds(0, 16 * (3 + 2 * (NZ - 1)))], 9)
    left_here(xbuf.at[pl.ds(0, 512)], 10)
    left_here(xbuf.at[pl.ds(0, 16 * (NZ - 1))], 13)
    for k in range(NY):
        landed(tile(1 - c, 0, k, 128), sib_sem.at[k])


def body(matrix, signs, samples):
    vmem = pltpu.VMEM
    f32 = jnp.float32
    dma = pltpu.SemaphoreType.DMA
    spec = pl.BlockSpec(memory_space=pltpu.VMEM)
    return pl.pallas_call(
        kernel,
        out_shape=(
            jax.ShapeDtypeStruct((64, 256), f32),
            jax.ShapeDtypeStruct((256, 1024), f32),
        ),
        in_specs=[pl.BlockSpec(memory_space=pltpu.HBM)] * 3,
        out_specs=(spec, spec),
        scratch_shapes=[
            vmem((BLOCK, 256), f32),
            vmem((BLOCK, 256), f32),
            vmem((4 * BLOCK, LANES), f32),
            vmem((CHIPS, SHARE), jnp.int32),
            vmem((CHIPS, SHARE), jnp.int32),
            vmem((CHIPS, SHARE), jnp.int32),
            pltpu.SMEM((CHIPS, SHARE), jnp.int32),
            vmem((CHIPS * YROWS, LANES), f32),
            vmem((CHIPS * YROWS, LANES), f32),
            vmem((CHIPS * YROWS, LANES), f32),
            vmem((CHIPS * ZROWS, LANES), f32),
            vmem((CHIPS * ZROWS, LANES), f32),
            vmem((CHIPS * ZROWS, LANES), f32),
            vmem((NY * NZ * YROWS, LANES), f32),
            vmem((NZ * YROWS, LANES), f32),
            vmem((7 * NY * ZROWS, LANES), f32),
            vmem((NY * ZROWS, LANES), f32),
            vmem((SHARE, LANES), f32),
            vmem((NY * SHARE, LANES), f32),
            vmem((2 * NY * SHARE, LANES), f32),
            vmem((64, LANES), f32),
            vmem((SHARE, 256), f32),
            vmem((SHARE, 256), f32),
            dma((BLOCK // CHUNK,)),
            dma((3,)),
            dma((CHIPS,)),
            dma((NZ,)),
            dma((NY, NZ)),
            dma((NZ,)),
            dma((7,)),
            dma((NY,)),
            dma,
            dma((NY,)),
            dma((NY,)),
            dma((NY,)),
            dma((NZ,)),
            dma((NZ,)),
            dma((NZ,)),
            dma((NY, NZ)),
            dma((NY,)),
            dma((14,)),
        ],
        compiler_params=pltpu.CompilerParams(
            collective_id=0, has_side_effects=True, vmem_limit_bytes=62 * 2**20
        ),
    )(matrix, signs.reshape(CHIPS, SHARE), samples.reshape(CHIPS, SHARE))


def solution(mesh):
    return jax.shard_map(
        body,
        mesh=mesh,
        in_specs=(P("row", "col"), P("row"), P()),
        out_specs=(P("row", "col"), P("col", None)),
        check_vma=False,
    )
```

time: 70.8 us -> 69.7 us (0.984)
  local copies, waits for them, and re-layouts: 5.22 us -> 3.78 us
    unnamed x8 -> x2, local copies, waits for them, and re-layouts: 5.22 us -> 3.78 us
where the time goes in v2:
time: 69.7 us; the launch traced here: 69.5 us
  Pallas kernels  65.1 us (93%)
  local copies, waits for them, and re-layouts  3.78 us (5%)
    pallas_call x1, Pallas kernels, body(): pl.pallas_call(kernel, out_shape=(jax.ShapeDtypeStruct((64, 256), f32), j...  65.1 us
    unnamed x2, local copies, waits for them, and re-layouts  3.78 us

profile of v2, /device:TPU:1, one launch (start us, length us, event | category | flops | bytes accessed | tf_op | source)
XLA Modules:
  0.0 69.5 jit_solution(988398128129354636)
XLA Ops:
  0.6 65.1 %shard_map.50 = (f32[64,256]{1,0:T(8,128)}, f32[256,1024]{1,0:T(8,128)}) custom-call(f32[4096,256]{1,0:T(8,128)} %matrix.1, s32[32,128]{1,0:T(8,128)} %bitcast.2, s32[32,128]{1,0:T(8,128)} %bitcast.3), custom_call_target="tpu_custom_call" | custom-call | tf_op jit(solution)/shard_map/pallas_call | solution.py:443
  65.7 1.5 %copy.7 = f32[64,256]{1,0:T(8,128)} copy(f32[64,256]{1,0:T(8,128)} %get-tuple-element.4) | data formatting | bytes 131072
  67.2 2.3 %copy.8 = f32[256,1024]{1,0:T(8,128)} copy(f32[256,1024]{1,0:T(8,128)} %get-tuple-element.5) | data formatting | bytes 2097152

commit v3 on v2

--- a/solution.py
+++ b/solution.py
@@ -14,10 +14,10 @@
 SHARE = 128
 LANES = 128
 CHUNK = 512
-YROWS = 104
+YROWS = 88
 ZROWS = SHARE - YROWS
 FINISH = 4
-PICK_Z, MERGE_Z, SECOND_Z, THIRD_Z = 1, 2, 5, 8
+SECOND_Z, THIRD_Z = 5, 9
 
 
 def device(x, y, z, c):
@@ -46,7 +46,7 @@
 
 
 def kernel(
-    matrix, signs_in, samples_in, sketch, gram,
+    matrix, whole_in, sketch, gram,
     xbuf, ybuf, table, signs, samples, picks, places,
     mine, other, theirs, minez, otherz, theirsz,
     ypart, zpart, zin, yin, total, left, right, skin, block, zgram,
@@ -82,8 +82,8 @@
     def greet(where):
         pl.semaphore_signal(barrier, inc=1, device_id=where, device_id_type=MESH)
 
-    get_signs = pltpu.make_async_copy(signs_in, signs, place_sem.at[0])
-    get_samples = pltpu.make_async_copy(samples_in, samples, place_sem.at[1])
+    get_signs = pltpu.make_async_copy(whole_in.at[pl.ds(CHIPS, CHIPS)], signs, place_sem.at[0])
+    get_samples = pltpu.make_async_copy(whole_in.at[pl.ds(0, CHIPS)], samples, place_sem.at[1])
     get_samples.start()
     get_signs.start()
     for i in range(BLOCK // CHUNK):
@@ -220,32 +220,26 @@
         def _():
             send(mine.at[own], zpart.at[part_y(p)], z_sem.at[p], at_z(stride(p)), 2)
 
-    def pick_z():
-        def each(p, _):
-            zz = z_of(p)
-            for yy in range(NY):
-                gather(chunk(yy, zz), YROWS, ZROWS, minez, otherz, (zz * NY + yy) * ZROWS)
-            send(otherz.at[part_z(zz)], theirsz.at[part_z(zz)], corez_sem.at[zz], sibling, 0)
-            return 0
-
-        lax.fori_loop(0, NZ, each, 0)
-
-    def send_z(step, slot, hop):
-        send(minez.at[part_z(turn_z(step))], zin.at[part_z(slot)], zin_sem.at[slot], at_z(hop), 11)
-
-    def merge_z():
-        def each(p, _):
-            zz = z_of(p)
-            landed(theirsz.at[part_z(zz)], corez_sem.at[zz])
-            minez[part_z(zz), :] += theirsz[part_z(zz), :]
-            return 0
-
-        lax.fori_loop(0, NZ, each, 0)
-        send_z(4, 0, 2 * ahead)
-        send_z(3 * ahead, 1, ahead)
-        send_z(-3 * ahead, 2, -ahead)
-        send_z(ahead, 3, ahead)
-        send_z(-ahead, 4, -ahead)
+    def pick_z(p):
+        zz = z_of(p)
+        for yy in range(NY):
+            gather(chunk(yy, zz), YROWS, ZROWS, minez, otherz, (zz * NY + yy) * ZROWS)
+        send(otherz.at[part_z(zz)], theirsz.at[part_z(zz)], corez_sem.at[zz], sibling, 0)
+
+    def send_z(zz, slot, hop):
+        send(minez.at[part_z(zz)], zin.at[part_z(slot)], zin_sem.at[slot], at_z(hop), 11)
+
+    def merge_z(p):
+        zz = z_of(p)
+        landed(theirsz.at[part_z(zz)], corez_sem.at[zz])
+        minez[part_z(zz), :] += theirsz[part_z(zz), :]
+        way = 2 * (p % 2) - 1
+        hop = jnp.where(p == 0, 2 * ahead, way)
+        slot = jnp.where(p == 0, 0, jnp.where(p < 3, 1, 3) + (1 - way * ahead) // 2)
+
+        @pl.when(jnp.logical_or(p < 3, jnp.logical_or(p == 5, p == 6)))
+        def _():
+            send_z(zz, slot, hop)
 
     def take_z(step, slots):
         zz = turn_z(step)
@@ -255,9 +249,9 @@
 
     def second_z():
         take_z(2 * ahead, (0, 1))
-        send_z(2 * ahead, 5, 2 * ahead)
+        send_z(turn_z(2 * ahead), 5, 2 * ahead)
         take_z(-2 * ahead, (2,))
-        send_z(-2 * ahead, 6, -2 * ahead)
+        send_z(turn_z(-2 * ahead), 6, -2 * ahead)
 
     def third_z():
         take_z(0, (3, 4, 5, 6))
@@ -269,26 +263,22 @@
     pick(0)
     pl.semaphore_wait(barrier, NZ + NY + NX - 2)
     give(0)
+    pick_z(0)
     pick(1)
     give(1)
+    pick_z(1)
 
     def turn(t, _):
         @pl.when(t < NZ)
         def _():
             merge(t)
+            merge_z(t)
 
         @pl.when(t < NZ - 2)
         def _():
             pick(t + 2)
             give(t + 2)
-
-        @pl.when(t == PICK_Z)
-        def _():
-            pick_z()
-
-        @pl.when(t == MERGE_Z)
-        def _():
-            merge_z()
+            pick_z(t + 2)
 
         @pl.when(t == SECOND_Z)
         def _():
@@ -352,21 +342,30 @@
         out += lax.dot_general(llow, rhigh, dims, preferred_element_type=jnp.float32)
         block[:, pl.ds(pl.multiple_of(h * LANES, LANES), LANES)] = out * (1.0 / 4096.0)
 
+    def strip(zz):
+        return rows(zz * 16, 16)
+
+    def pass_on(h, turn):
+        lanes = pl.ds(pl.multiple_of(h * LANES, LANES), LANES)
+        for p in range(NZ - 1):
+            send(
+                block.at[strip(z_of(p)), lanes], zgram.at[strip(p), lanes],
+                rs_sem.at[turn, p], at_z(stride(p)), 7,
+            )
+
     product(c)
+    pass_on(c, 0)
     landed(skin, sk_sem)
     sketch[:, pl.ds(pl.multiple_of((1 - c) * LANES, LANES), LANES)] = skin[...]
     for k in range(NY):
         landed(right.at[part_of((1 - c) * NY + k)], fwd_sem.at[k])
     product(1 - c)
-
-    def strip(zz):
-        return rows(zz * 16, 16)
-
-    for p in range(NZ - 1):
-        send(block.at[strip(z_of(p))], zgram.at[strip(p)], rs_sem.at[p], at_z(stride(p)), 7)
+    pass_on(1 - c, 1)
+
     acc = block[strip(z), :]
     for p in range(NZ - 2, -1, -1):
-        landed(zgram.at[strip(p)], rs_sem.at[p])
+        landed(zgram.at[strip(p), pl.ds(0, LANES)], rs_sem.at[0, p])
+        landed(zgram.at[strip(p), pl.ds(0, LANES)], rs_sem.at[1, p])
         acc = acc + zgram[strip(p), :]
 
     def tile(cc, zz, yy, count):
@@ -446,7 +445,7 @@
             jax.ShapeDtypeStruct((64, 256), f32),
             jax.ShapeDtypeStruct((256, 1024), f32),
         ),
-        in_specs=[pl.BlockSpec(memory_space=pltpu.HBM)] * 3,
+        in_specs=[pl.BlockSpec(memory_space=pltpu.HBM)] * 2,
         out_specs=(spec, spec),
         scratch_shapes=[
             vmem((BLOCK, 256), f32),
@@ -484,7 +483,7 @@
             dma((NY,)),
             dma((NY,)),
             dma((NY,)),
-            dma((NZ,)),
+            dma((2, NZ)),
             dma((NZ,)),
             dma((NZ,)),
             dma((NY, NZ)),
@@ -492,9 +491,9 @@
             dma((14,)),
         ],
         compiler_params=pltpu.CompilerParams(
-            collective_id=0, has_side_effects=True, vmem_limit_bytes=62 * 2**20
+            collective_id=0, has_side_effects=True, vmem_limit_bytes=52 * 2**20
         ),
-    )(matrix, signs.reshape(CHIPS, SHARE), samples.reshape(CHIPS, SHARE))
+    )(matrix, jnp.concatenate([samples, signs]).reshape(2 * CHIPS, SHARE))
 
 
 def solution(mesh):

time: 69.7 us -> 63.9 us (0.917)
  Pallas kernels: 65.1 us -> 60.7 us
  local copies, waits for them, and re-layouts: 3.78 us -> 1.6 us
  other arithmetic: 0 us -> 0.74 us
    pallas_call x1, Pallas kernels: 65.1 us -> 60.7 us  [body(): pl.pallas_call(kernel, out_shape=(jax.ShapeDtypeStruct((64, 256), f32), j...]
    unnamed x2, local copies, waits for them, and re-layouts: 3.78 us -> 1.6 us
    concatenate x0 -> x1, other arithmetic: none -> 0.74 us  [body(): jnp.concatenate([samples, signs]).reshape(2 * CHIPS, SHARE)]
where the time goes in v3:
time: 63.9 us; the launch traced here: 63.6 us
  Pallas kernels  60.7 us (95%)
  local copies, waits for them, and re-layouts  1.6 us (3%)
  other arithmetic  0.74 us (1%)
  between operations  0.64 us (1%)
    pallas_call x1, Pallas kernels, body(): pl.pallas_call(kernel, out_shape=(jax.ShapeDtypeStruct((64, 256), f32), j...  60.7 us
    unnamed x2, local copies, waits for them, and re-layouts  1.6 us

profile of v3, /device:TPU:1, one launch (start us, length us, event | category | flops | bytes accessed | tf_op | source)
XLA Modules:
  0.0 63.6 jit_solution(17247441075696805124)
XLA Ops:
  0.6 0.7 %pad_add_fusion.whole_in = s32[64,128]{1,0:T(8,128)S(1)} fusion(s32[32,128]{1,0:T(8,128)} %bitcast.2, s32[32,128]{1,0:T(8,128)} %bitcast.3), kind=kLoop, calls=%fused_computation | loop fusion | flops 8192 | bytes 65536 | tf_op jit(solution)/shard_map/concatenate | solution.py:496
  1.4 60.7 %shard_map.50 = (f32[64,256]{1,0:T(8,128)S(1)}, f32[256,1024]{1,0:T(8,128)S(1)}) custom-call(f32[4096,256]{1,0:T(8,128)} %matrix.1, s32[64,128]{1,0:T(8,128)S(1)} %pad_add_fusion.whole_in), custom_call_target="tpu_custom_call" | custom-call | tf_op jit(solution)/shard_map/pallas_call | solution.py:442
  62.0 0.6 copy.7
  62.7 1.0 %copy.8 = f32[256,1024]{1,0:T(8,128)} copy(f32[256,1024]{1,0:T(8,128)S(1)} %get-tuple-element.5) | data formatting | bytes 2097152

commit v4 on v3

--- a/solution.py
+++ b/solution.py
@@ -203,12 +203,16 @@
             spot = chunk(y_of(q), z_of(p))
             landed(theirs.at[part_y(spot)], core_sem.at[spot])
             mine[part_y(spot), :] += theirs[part_y(spot), :]
+            k = (2 + q) % NY
+
+            @pl.when(k != 0)
+            def _():
+                slot = k * NZ + p
+                send(mine.at[part_y(spot)], ypart.at[part_y(slot)], ypart_sem.at[k, p], at_y(k), 1)
+
             return 0
 
         lax.fori_loop(0, 4, each, 0)
-        for k in (2, 1, 3):
-            spot = chunk((y + k) % NY, z_of(p))
-            send(mine.at[part_y(spot)], ypart.at[part_y(k * NZ + p)], ypart_sem.at[k, p], at_y(k), 1)
 
     def finish(p):
         own = part_y(chunk(y, z_of(p)))
@@ -264,8 +268,6 @@
     pl.semaphore_wait(barrier, NZ + NY + NX - 2)
     give(0)
     pick_z(0)
-    pick(1)
-    give(1)
     pick_z(1)
 
     def turn(t, _):
@@ -273,6 +275,11 @@
         def _():
             merge(t)
             merge_z(t)
+
+        @pl.when(t == 0)
+        def _():
+            pick(1)
+            give(1)
 
         @pl.when(t < NZ - 2)
         def _():

time: 63.9 us -> 64.6 us (1.011)
    pallas_call x1, Pallas kernels: 60.7 us -> 61.3 us  [body(): pl.pallas_call(kernel, out_shape=(jax.ShapeDtypeStruct((64, 256), f32), j...]
where the time goes in v4:
time: 64.6 us; the launch traced here: 64.3 us
  Pallas kernels  61.3 us (95%)
  local copies, waits for them, and re-layouts  1.6 us (2%)
  other arithmetic  0.74 us (1%)
    pallas_call x1, Pallas kernels, body(): pl.pallas_call(kernel, out_shape=(jax.ShapeDtypeStruct((64, 256), f32), j...  61.3 us
    unnamed x2, local copies, waits for them, and re-layouts  1.6 us

profile of v4, /device:TPU:1, one launch (start us, length us, event | category | flops | bytes accessed | tf_op | source)
XLA Modules:
  0.0 64.3 jit_solution(14878033617025576016)
XLA Ops:
  0.6 0.7 %pad_add_fusion.whole_in = s32[64,128]{1,0:T(8,128)S(1)} fusion(s32[32,128]{1,0:T(8,128)} %bitcast.2, s32[32,128]{1,0:T(8,128)} %bitcast.3), kind=kLoop, calls=%fused_computation | loop fusion | flops 8192 | bytes 65536 | tf_op jit(solution)/shard_map/concatenate | solution.py:503
  1.4 61.3 %shard_map.50 = (f32[64,256]{1,0:T(8,128)S(1)}, f32[256,1024]{1,0:T(8,128)S(1)}) custom-call(f32[4096,256]{1,0:T(8,128)} %matrix.1, s32[64,128]{1,0:T(8,128)S(1)} %pad_add_fusion.whole_in), custom_call_target="tpu_custom_call" | custom-call | tf_op jit(solution)/shard_map/pallas_call | solution.py:449
  62.7 0.6 copy.7
  63.4 1.0 %copy.8 = f32[256,1024]{1,0:T(8,128)} copy(f32[256,1024]{1,0:T(8,128)S(1)} %get-tuple-element.5) | data formatting | bytes 2097152
